TPU v7x, 256 devices: a whole 4x4x8 slice. The times are simulated.
256 devices in a mesh: dp: 32 (over z, y), tensor: 8 (over x, core).
Axes of the slice: x: 4, y: 4, z: 8, core: 2. Of those that a mesh axis runs over, the one named last changes fastest.
Arguments:
- hidden_in: bfloat16 [65536, 14336], P('dp', 'tensor'), may hold values from -6 to 6
- out_grad: bfloat16 [65536, 4096], P('dp', 'tensor'), may hold values from -6 to 6
- proj_in: bfloat16 [14336, 64], P('tensor'), may hold values from -0.046875 to 0.046875
- proj_out: bfloat16 [4096, 64], P('tensor'), may hold values from -0.09375 to 0.09375
- token_mask: int32 [65536], P('dp'), may hold values 0 or 1
- cand_ids: int32 [32], P('dp'), may hold values from 0 to 1023
- queries: bfloat16 [1024, 4096], P('tensor', 'dp'), may hold values from -6 to 6
Outputs:
- scores: float32 [32, 1024], P('dp', 'tensor')
All inputs are finite; a program needn't handle non-finite values. No bound on the sum of `token_mask` on one device may be relied on, other than what follows from the above.
Results may differ from a plain program's by a relative error of at most 0.0029.
Values may be sent and summed in bfloat16 or wider, within the bound.
No kernel may reach another device: no remote copies, remote signals or barrier semaphores. Data moves between devices by JAX's collectives and lax.ppermute only.
A program may use at most 64 MiB of HBM per device.

v0:
```python
import jax
import jax.numpy as jnp
from jax import lax
from jax.sharding import PartitionSpec as P


def body(hidden_in, out_grad, proj_in, proj_out, token_mask, cand_ids, queries):
    rank = proj_in.shape[1]
    entries = rank * rank
    xp_part = jnp.dot(hidden_in, proj_in, preferred_element_type=jnp.float32)
    gp_part = jnp.dot(out_grad, proj_out, preferred_element_type=jnp.float32)
    weights = token_mask.astype(jnp.float32)
    xp_full, gp_full = lax.psum((xp_part, gp_part), "tensor")
    outer = jnp.dot((gp_full * weights[:, None]).T, xp_full, precision=lax.Precision.HIGHEST)
    flat = outer.reshape(1, entries)
    grms = jnp.sqrt(jnp.mean(flat * flat, axis=1, keepdims=True) + 1e-06)
    unit = (flat / grms).astype(jnp.bfloat16)
    qlocal = queries.shape[0]
    piece = lax.all_gather(queries, "dp", axis=1, tiled=True)
    dots = lax.dot_general(
        unit, piece, (((1,), (1,)), ((), ())), preferred_element_type=jnp.float32
    )
    pfloat = piece.astype(jnp.float32)
    squares = jnp.sum(pfloat * pfloat, axis=1)
    dots, squares = (dots, squares)
    qrms = jnp.sqrt(squares / entries + 1e-06)
    scores = dots / (rank * qrms[None, :])
    index = lax.axis_index("tensor") * qlocal + jnp.arange(qlocal, dtype=jnp.int32)
    return jnp.where(index[None, :] == cand_ids[:, None], jnp.float32(0.0), scores)


def solution(mesh):
    placed = (
        P("dp", "tensor"),
        P("dp", "tensor"),
        P("tensor", None),
        P("tensor", None),
        P("dp"),
        P("dp"),
        P("tensor", "dp"),
    )
    return jax.shard_map(
        body, mesh=mesh, in_specs=placed, out_specs=P("dp", "tensor"), check_vma=False
    )
```

profile of v0, /device:TPU:56, one launch (start us, length us, event | category | flops | bytes accessed | tf_op | source)
XLA Modules:
  0.0 107.9 jit_solution(13204708081158973739)
XLA Ops:
  7.4 0.0 copy-start
  7.4 0.0 copy-start.1
  7.4 0.0 all-reduce.3.cloned.1.call-start
  7.4 1.6 %copy-done = bf16[2048,512]{1,0:T(8,128)(2,1)S(1)} copy-done((bf16[2048,512]{1,0:T(8,128)(2,1)S(1)}, bf16[2048,512]{1,0:T(8,128)(2,1)}, u32[]{:S(2)}) %copy-start) | copy-done | bytes 2097176
  9.0 2.5 %fusion.6 = f32[2048,64]{1,0:T(8,128)} fusion(bf16[2048,512]{1,0:T(8,128)(2,1)S(1)} %copy-done, bf16[512,64]{0,1:T(8,128)(2,1)} %param.10), kind=kOutput, calls=%fused_computation.10 | convolution fusion | flops 134217728 | bytes 2686976 | tf_op jit(solution)/shard_map/dot_general | solution.py:11
  11.5 0.0 copy-done.1
  11.5 6.1 %fusion.7 = f32[2048,64]{1,0:T(8,128)} fusion(bf16[2048,1792]{1,0:T(8,128)(2,1)} %param.7, bf16[1792,64]{0,1:T(8,128)(2,1)S(1)} %copy-done.1), kind=kOutput, calls=%fused_computation.11 | convolution fusion | flops 469762048 | bytes 8093696 | tf_op jit(solution)/shard_map/dot_general | solution.py:10
  17.6 0.0 copy-start.2
  17.6 0.0 all-reduce.3.cloned.1.call-update
  17.6 0.0 all-gather.2.cloned.1.call-start
  17.7 0.5 all-gather.2.cloned.1.call-update
  18.2 0.1 copy-done.2
  18.9 72.7 %all-reduce.3.cloned.1.call-done = (f32[2048,64]{1,0:T(8,128)}, f32[2048,64]{1,0:T(8,128)}) async-done(((f32[2048,64]{1,0:T(8,128)}, f32[2048,64]{1,0:T(8,128)}), (f32[2048,64]{1,0:T(8,128)}, f32[2048,64]{1,0:T(8,128)})) %all-reduce.3.cloned.1.call-update) | async-done | bytes 1048592 | tf_op jit(solution)/shard_map/psum | solution.py:13
  91.6 4.4 %multiply_reduce_fusion.1 = (f32[]{:T(128)}, f32[64,64]{1,0:T(8,128)S(1)}) fusion(f32[2048,64]{1,0:T(8,128)} %get-tuple-element.5, f32[2048,64]{1,0:T(8,128)} %get-tuple-element.6, f32[2048]{0:T(1024)S(1)} %convert_element_type.15), kind=kOutput, calls=%fused_computation.9 | convolution fusion | flops 100802560 | bytes 1073156 | tf_op jit(solution)/shard_map/dot_general | solution.py:14
  96.7 0.1 reshape.32
  96.8 0.0 all-gather.2.cloned.1.call-done
  96.8 1.5 %multiply_reduce_fusion = f32[128]{0:T(128)S(1)} fusion(bf16[128,4096]{1,0:T(8,128)(2,1)} %all-gather.2.cloned.1.call-done), kind=kLoop, calls=%fused_computation | loop fusion | flops 1572736 | bytes 1049088 | tf_op jit(solution)/shard_map/reduce_sum | solution.py:24
  98.3 2.1 %fusion.2 = f32[1,128]{1,0:T(1,128)} fusion(bf16[4096,1]{0,1:T(2,128)(2,1)S(1)} %reshape.32, bf16[128,4096]{1,0:T(8,128)(2,1)} %all-gather.2.cloned.1.call-done, f32[128]{0:T(128)S(1)} %multiply_reduce_fusion, s32[]{:T(128)} %bitcast.18, s32[]{:T(128)S(6)} %mul.27), kind=kOutput, calls=%fused_computation.4 | convolution fusion | flops 1049472 | bytes 1057800 | tf_op jit(solution)/shard_map/dot_general | solution.py:20
  (2 shorter events, 0.0 us)
Async XLA Ops:
  7.4 1.6 %copy-start = (bf16[2048,512]{1,0:T(8,128)(2,1)S(1)}, bf16[2048,512]{1,0:T(8,128)(2,1)}, u32[]{:S(2)}) copy-start(bf16[2048,512]{1,0:T(8,128)(2,1)} %param.8) | copy-start | bytes 6291460
  7.4 4.1 %copy-start.1 = (bf16[1792,64]{0,1:T(8,128)(2,1)S(1)}, bf16[1792,64]{0,1:T(8,128)(2,1)}, u32[]{:S(2)}) copy-start(bf16[1792,64]{0,1:T(8,128)(2,1)} %param.9) | copy-start | bytes 688132
  7.4 84.2 %all-reduce.3.cloned.1.call-start = ((), (), s32[]{:S(2)}) async-start(), calls=%async_computation.1 | async-start | bytes 4194304 | tf_op jit(solution)/shard_map/psum | solution.py:13
  17.6 0.7 copy-start.2
  17.6 79.2 %all-gather.2.cloned.1.call-start = ((), (), s32[]{:S(2)}) async-start(), calls=%async_computation | async-start | bytes 1081344 | tf_op jit(solution)/shard_map/all_gather | solution.py:19
Sparse Core Ops, SparseCore 0:
  17.7 73.8 all-reduce.2
Sparse Core Ops, SparseCore 1:
  20.6 73.4 all-gather.1
where the time goes:
time: 109 us; the launch traced here: 108 us
  waiting for transfers between devices  73.2 us (67%)
  between operations  16.2 us (15%)
  matrix products  15.1 us (14%)
  local copies, waits for them, and re-layouts  1.77 us (2%)
  other arithmetic  1.53 us (1%)
    psum x1, waiting for transfers between devices, body(): xp_full, gp_full = lax.psum((xp_part, gp_part), 'tensor')  72.7 us
    dot_general x1, matrix products, body(): xp_part = jnp.dot(hidden_in, proj_in, preferred_element_type=jnp.float32)  6.12 us
    dot_general x1, matrix products, body(): jnp.dot((gp_full * weights[:, None]).T, xp_full, precision=lax.Precision....  4.38 us
    dot_general x1, matrix products, body(): gp_part = jnp.dot(out_grad, proj_out, preferred_element_type=jnp.float32)  2.5 us
  transfers between devices with their start and end apart: 2, of which 1 were waited for; matrix products, arithmetic and copies ran while one was open for 4% of the time, Pallas kernels for 0%

commit v1 on v0

v1 whole, which is shorter than its diff:
```python
import functools

import jax
import jax.numpy as jnp
from jax import lax
from jax.experimental import pallas as pl
from jax.experimental.pallas import tpu as pltpu
from jax.sharding import PartitionSpec as P

BLOCK = 256
PROJECT_VMEM = 61 << 20
SMALL_VMEM = 8 << 20
ROWS = 4
HIGHEST = lax.Precision.HIGHEST


def nt_dot(a, b, precision=None):
    return lax.dot_general(
        a, b, (((1,), (1,)), ((), ())), preferred_element_type=jnp.float32, precision=precision
    )


def project_kernel(place_ref, hidden_ref, grad_ref, pin_ref, pout_ref, out_ref, w_ref):
    rank, width = pin_ref.shape

    @pl.when(pl.program_id(0) == 0)
    def _():
        w_ref[...] = jnp.zeros_like(w_ref)
        w_ref[:rank, :width] = pin_ref[...]
        w_ref[rank:, width:] = pout_ref[...]

    out_ref[...] = nt_dot(hidden_ref[...], w_ref[:, :width]) + nt_dot(grad_ref[...], w_ref[:, width:])


def project(place, hidden, grad, pin_t, pout_t):
    rank, width = pin_t.shape
    depth = pout_t.shape[1]
    rows = hidden.shape[0] // 2
    steps = rows // BLOCK

    def tokens(k, place_ref):
        return place_ref[0] * steps + jnp.bitwise_xor(place_ref[1], k), 0

    def whole(k, place_ref):
        return 0, 0

    return pl.pallas_call(
        project_kernel,
        out_shape=jax.ShapeDtypeStruct((rows, 2 * rank), jnp.float32),
        grid_spec=pltpu.PrefetchScalarGridSpec(
            num_scalar_prefetch=1,
            grid=(steps,),
            in_specs=[
                pl.BlockSpec((BLOCK, width), tokens),
                pl.BlockSpec((BLOCK, depth), tokens),
                pl.BlockSpec((rank, width), whole),
                pl.BlockSpec((rank, depth), whole),
            ],
            out_specs=pl.BlockSpec((BLOCK, 2 * rank), lambda k, place_ref: (k, 0)),
            scratch_shapes=[pltpu.VMEM((2 * rank, width + depth), jnp.bfloat16)],
        ),
        compiler_params=pltpu.CompilerParams(vmem_limit_bytes=PROJECT_VMEM),
        cost_estimate=pl.CostEstimate(
            flops=2 * rows * (width + depth) * 256, bytes_accessed=2 * rows * (width + depth), transcendentals=0
        ),
        name="project",
    )(place, hidden, grad, pin_t, pout_t)


def pair_kernel(a_ref, b_ref, *outs):
    for k, out in enumerate(outs):
        rows = pl.ds(k * BLOCK, BLOCK)
        out[...] = a_ref[rows, :] + b_ref[rows, :]


def pair_sum(a, b):
    n = a.shape[0] // BLOCK
    vmem = pl.BlockSpec(memory_space=pltpu.VMEM)
    return pl.pallas_call(
        pair_kernel,
        out_shape=[jax.ShapeDtypeStruct((BLOCK, a.shape[1]), jnp.float32)] * n,
        in_specs=[vmem] * 2,
        out_specs=[vmem] * n,
        compiler_params=pltpu.CompilerParams(vmem_limit_bytes=SMALL_VMEM),
        name="pair_sum",
    )(a, b)


def outer_kernel(first_ref, mask_ref, *refs):
    parts, out_ref, tmp_ref = refs[:-2], refs[-2], refs[-1]
    mask = mask_ref[pl.ds(first_ref[0], 1), :].astype(jnp.float32)
    total = functools.reduce(lambda a, b: a + b, [r[...] for r in parts])
    rank = total.shape[1] // 2
    masked = total.T[rank:, :] * mask
    tmp_ref[...] = lax.dot_general(
        masked, total, (((1,), (0,)), ((), ())), preferred_element_type=jnp.float32, precision=HIGHEST
    )
    even = tmp_ref[pl.ds(0, rank // 2, stride=2), :]
    odd = tmp_ref[pl.ds(1, rank // 2, stride=2), :]
    out_ref[...] = jnp.concatenate([even[:, :rank], odd[:, :rank]], axis=1)


def outer(first, mask, parts):
    vmem = pl.BlockSpec(memory_space=pltpu.VMEM)
    rank = parts[0].shape[1] // 2
    return pl.pallas_call(
        outer_kernel,
        out_shape=jax.ShapeDtypeStruct((rank // 2, 2 * rank), jnp.float32),
        in_specs=[pl.BlockSpec(memory_space=pltpu.SMEM)] + [vmem] * (1 + len(parts)),
        out_specs=vmem,
        scratch_shapes=[pltpu.VMEM((rank, 2 * rank), jnp.float32)],
        compiler_params=pltpu.CompilerParams(vmem_limit_bytes=SMALL_VMEM),
        name="outer",
    )(first, mask, *parts)


def sum_kernel(*refs):
    refs[-1][...] = functools.reduce(lambda a, b: a + b, [r[...] for r in refs[:-1]])


def sum_parts(parts):
    vmem = pl.BlockSpec(memory_space=pltpu.VMEM)
    return pl.pallas_call(
        sum_kernel,
        out_shape=jax.ShapeDtypeStruct(parts[0].shape, jnp.float32),
        in_specs=[vmem] * len(parts),
        out_specs=vmem,
        compiler_params=pltpu.CompilerParams(vmem_limit_bytes=SMALL_VMEM),
        name="sum_parts",
    )(*parts)


def score_kernel(rank, ids_ref, a_ref, b_ref, *refs):
    q_refs, out_ref, unit_ref = refs[:-2], refs[-2], refs[-1]
    grad = a_ref[...] + b_ref[...]
    entries = grad.size
    mean = jnp.sum(grad * grad, keepdims=True) / entries
    unit_ref[...] = (grad / jnp.sqrt(mean + 1e-06)).astype(jnp.bfloat16).astype(jnp.float32)
    layers, qlocal, lanes = q_refs[0].shape
    dots = jnp.zeros((qlocal, lanes), jnp.float32)
    squares = jnp.zeros((qlocal, lanes), jnp.float32)
    for z in range(layers):
        for k, q_ref in enumerate(q_refs):
            q = q_ref[z].astype(jnp.float32)
            row = z * len(q_refs) + jnp.bitwise_xor(ids_ref[2], k)
            dots += q * unit_ref[pl.ds(row, 1), :]
            squares += q * q
    ones = jnp.ones((8, lanes), jnp.float32)
    dots = nt_dot(ones, dots, HIGHEST)[:1]
    squares = nt_dot(ones, squares, HIGHEST)[:1]
    scores = dots / (rank * jnp.sqrt(squares / entries + 1e-06))
    index = ids_ref[1] + lax.broadcasted_iota(jnp.int32, scores.shape, 1)
    out_ref[...] = jnp.where(index == ids_ref[0], 0.0, scores)


def score(rank, ids, a, b, q):
    vmem = pl.BlockSpec(memory_space=pltpu.VMEM)
    return pl.pallas_call(
        functools.partial(score_kernel, rank),
        out_shape=jax.ShapeDtypeStruct((1, q[0].shape[1]), jnp.float32),
        in_specs=[pl.BlockSpec(memory_space=pltpu.SMEM)] + [vmem] * (2 + len(q)),
        out_specs=vmem,
        scratch_shapes=[pltpu.VMEM(a.shape, jnp.float32)],
        compiler_params=pltpu.CompilerParams(vmem_limit_bytes=SMALL_VMEM),
        name="score",
    )(ids, a, b, *q)


def body(hidden_in, out_grad, proj_in, proj_out, token_mask, cand_ids, queries):
    rank = proj_in.shape[1]
    devices = lax.axis_size("tensor")
    chips = devices // 2
    dp = lax.axis_size("dp")
    me = lax.axis_index("tensor").astype(jnp.int32)
    core, chip = me % 2, me // 2
    qlocal, qcols = queries.shape

    def swap(x, mask):
        return lax.ppermute(x, "tensor", [(i, i ^ mask) for i in range(devices)])

    with jax.named_scope("gather_queries"):
        layers = dp // ROWS
        columns = [[z * ROWS + y for z in range(layers)] for y in range(ROWS)]
        copies = jnp.broadcast_to(queries[None], (layers, qlocal, qcols))
        column = lax.all_to_all(copies, "dp", 0, 0, tiled=True, axis_index_groups=columns)
        gathered = [column] + [
            lax.ppermute(column, "dp", [(i, i ^ k) for i in range(dp)]) for k in range(1, ROWS)
        ]

    pin_t, pout_t = proj_in.T, proj_out.T
    with jax.named_scope("project"):
        theirs = project(jnp.stack([1 - core, chip]), hidden_in, out_grad, pin_t, pout_t)
        arrived = swap(theirs, 1)
        mine = project(jnp.stack([core, chip]), hidden_in, out_grad, pin_t, pout_t)
    with jax.named_scope("exchange_tokens"):
        blocks = pair_sum(mine, arrived)
        parts = [blocks[0]] + [swap(blocks[k], 2 * k) for k in range(1, chips)]
    with jax.named_scope("outer"):
        first = (core * chips + chip)[None]
        partial = outer(first, token_mask.reshape(-1, BLOCK), parts)
    with jax.named_scope("exchange_grad"):
        half = sum_parts([partial] + [swap(partial, 2 * k) for k in range(1, chips)])
        other = swap(half, 1)
    with jax.named_scope("score"):
        row = lax.axis_index("dp").astype(jnp.int32) % ROWS
        ids = jnp.stack([cand_ids[0], me * qlocal, row])
        return score(rank, ids, half, other, gathered)


def solution(mesh):
    placed = (
        P("dp", "tensor"),
        P("dp", "tensor"),
        P("tensor", None),
        P("tensor", None),
        P("dp"),
        P("dp"),
        P("tensor", "dp"),
    )
    return jax.shard_map(
        body, mesh=mesh, in_specs=placed, out_specs=P("dp", "tensor"), check_vma=False
    )
```

time: 109 us -> 49.4 us (0.45)
  the two profiles are of different devices: /device:TPU:56 before, /device:TPU:1 now
where the time goes in v1:
time: 49.4 us; the launch traced here: 49 us
  starting transfers between devices  22.7 us (46%)
  Pallas kernels  13.3 us (27%)
  waiting for transfers between devices  9.18 us (19%)
  local copies, waits for them, and re-layouts  1.81 us (4%)
  other arithmetic  1.24 us (3%)
  between operations  0.7 us (1%)
    ppermute x8, starting transfers between devices, swap(): return lax.ppermute(x, 'tensor', [(i, i ^ mask) for i in range(devices)])  12.3 us
    pallas_call x2, Pallas kernels, project(): pl.pallas_call(project_kernel, out_shape=jax.ShapeDtypeStruct((rows, 2 *...  11.2 us
    ppermute x8, waiting for transfers between devices, swap(): return lax.ppermute(x, 'tensor', [(i, i ^ mask) for i in range(devices)])  8.05 us
    all_to_all x1, starting transfers between devices, body(): lax.all_to_all(copies, 'dp', 0, 0, tiled=True, axis_index_groups=columns)  6.45 us
    ppermute x3, starting transfers between devices, body(): lax.ppermute(column, 'dp', [(i, i ^ k) for i in range(dp)])  3.92 us
    pallas_call x1, Pallas kernels, score(): pl.pallas_call(functools.partial(score_kernel, rank), out_shape=jax.Shape...  1.77 us
    all_to_all x1, waiting for transfers between devices, body(): lax.all_to_all(copies, 'dp', 0, 0, tiled=True, axis_index_groups=columns)  1.12 us
    unnamed x6, local copies, waits for them, and re-layouts  1.05 us
  transfers between devices with their start and end apart: 12, of which 6 were waited for; matrix products, arithmetic and copies ran while one was open for 3% of the time, Pallas kernels for 12%

profile of v1, /device:TPU:1, one launch (start us, length us, event | category | flops | bytes accessed | tf_op | source)
XLA Modules:
  0.0 49.0 jit_solution(15266994857898649994)
XLA Ops:
  0.0 0.6 %pad_add_fusion.2.place_ref = s32[2]{0:T(128)} fusion(s32[1]{0:T(128)} %bitcast.7, s32[1]{0:T(128)} %bitcast.4), kind=kLoop, calls=%fused_computation.2 | loop fusion | flops 2 | bytes 16 | tf_op jit(solution)/shard_map/project/stack | solution.py:192
  0.6 5.6 %project.3 = f32[1024,128]{1,0:T(8,128)} custom-call(s32[2]{0:T(128)} %pad_add_fusion.2.place_ref, bf16[2048,1792]{1,0:T(8,128)(2,1)} %hidden_ref.3, bf16[2048,512]{1,0:T(8,128)(2,1)} %grad_ref.3, bf16[64,1792]{1,0:T(8,128)(2,1)} %bitcast.8, bf16[64,512]{1,0:T(8,128)(2,1)} %bitcast.10), custom_call_target="tpu_custom_call" | custom-call | flops 1207959552 | bytes 4718592 | tf_op jit(solution)/shard_map/project/project/pallas_call | solution.py:47
  6.1 3.2 %collective-permute-start = (f32[1024,128]{1,0:T(8,128)}, f32[1024,128]{1,0:T(8,128)S(1)}, u32[]{:S(2)}, u32[]{:S(2)}) collective-permute-start(f32[1024,128]{1,0:T(8,128)} %project.3), channel_id=1, source_target_pairs={{0,1},{1,0},{2,3},{3,2},{4,5},{5,4},{6,7},{7,6},{8,9},{9,8},{10,11... | collective-permute-start | bytes 1572872 | tf_op jit(solution)/shard_map/project/ppermute | solution.py:179
  9.4 0.8 %broadcast_in_dim.10 = bf16[8,128,128]{2,1,0:T(8,128)(2,1)} broadcast(bf16[128,128]{1,0:T(8,128)(2,1)S(1)} %copy-done.1), dimensions={1,2} | broadcast | bytes 294912 | tf_op jit(solution)/shard_map/gather_queries/broadcast_in_dim | solution.py:184
  10.1 6.4 %all-to-all-start = ((bf16[8,128,128]{2,1,0:T(8,128)(2,1)}), bf16[8,128,128]{2,1,0:T(8,128)(2,1)S(1)}, u32[]{:S(2)}, u32[]{:S(2)}) async-start(bf16[8,128,128]{2,1,0:T(8,128)(2,1)} %broadcast_in_dim.10), calls=%async_computation | async-start | bytes 524288 | tf_op jit(solution)/shard_map/gather_queries/all_to_all | solution.py:185
  16.6 0.6 %pad_add_fusion.1.place_ref = s32[2]{0:T(128)} fusion(s32[1]{0:T(128)} %bitcast.3, s32[1]{0:T(128)} %bitcast.4), kind=kLoop, calls=%fused_computation.1 | loop fusion | flops 2 | bytes 16 | tf_op jit(solution)/shard_map/project/stack | solution.py:194
  17.2 5.6 %project.2.a_ref = f32[1024,128]{1,0:T(8,128)} custom-call(s32[2]{0:T(128)} %pad_add_fusion.1.place_ref, bf16[2048,1792]{1,0:T(8,128)(2,1)} %hidden_ref.3, bf16[2048,512]{1,0:T(8,128)(2,1)} %grad_ref.3, bf16[64,1792]{1,0:T(8,128)(2,1)} %bitcast.9, bf16[64,512]{1,0:T(8,128)(2,1)} %bitcast.11), custom_call_target="tpu_custom_call" | custom-call | flops 1207959552 | bytes 4718592 | tf_op jit(solution)/shard_map/project/project/pallas_call | solution.py:47
  22.8 0.0 collective-permute-done.b_ref
  22.8 1.0 %copy-done = f32[1024,128]{1,0:T(8,128)S(1)} copy-done((f32[1024,128]{1,0:T(8,128)S(1)}, f32[1024,128]{1,0:T(8,128)}, u32[]{:S(2)}) %copy-start) | copy-done | bytes 524312
  23.8 0.1 pair_sum.1
  23.9 1.3 %collective-permute-start.1 = (f32[256,128]{1,0:T(8,128)S(1)}, f32[256,128]{1,0:T(8,128)S(1)}, u32[]{:S(2)}, u32[]{:S(2)}) collective-permute-start(f32[256,128]{1,0:T(8,128)S(1)} %get-tuple-element.10), channel_id=1, source_target_pairs={{0,2},{1,3},{2,0},{3,1},{4,6},{5,7},{6,4},{7,5},{8,10},{9,11},{10,... | collective-permute-start | bytes 393224 | tf_op jit(solution)/shard_map/exchange_tokens/ppermute | solution.py:179
  25.2 2.5 %collective-permute-start.2 = (f32[256,128]{1,0:T(8,128)S(1)}, f32[256,128]{1,0:T(8,128)S(1)}, u32[]{:S(2)}, u32[]{:S(2)}) collective-permute-start(f32[256,128]{1,0:T(8,128)S(1)} %get-tuple-element.11), channel_id=1, source_target_pairs={{0,4},{1,5},{2,6},{3,7},{4,0},{5,1},{6,2},{7,3},{8,12},{9,13},{10,... | collective-permute-start | bytes 393224 | tf_op jit(solution)/shard_map/exchange_tokens/ppermute | solution.py:179
  27.6 0.2 collective-permute-start.3
  27.8 1.1 %all-to-all-done.refs_0_ = bf16[8,128,128]{2,1,0:T(8,128)(2,1)S(1)} async-done(((bf16[8,128,128]{2,1,0:T(8,128)(2,1)}), bf16[8,128,128]{2,1,0:T(8,128)(2,1)S(1)}, u32[]{:S(2)}, u32[]{:S(2)}) %all-to-all-start) | async-done | bytes 262176 | tf_op jit(solution)/shard_map/gather_queries/all_to_all | solution.py:185
  29.0 2.7 %collective-permute-start.10 = (bf16[8,128,128]{2,1,0:T(8,128)(2,1)S(1)}, bf16[8,128,128]{2,1,0:T(8,128)(2,1)S(1)}, u32[]{:S(2)}, u32[]{:S(2)}) collective-permute-start(bf16[8,128,128]{2,1,0:T(8,128)(2,1)S(1)} %all-to-all-done.refs_0_), channel_id=1, source_target_pairs={{0,24},{8,16},{16,8},{24,0},{32,56},{40,48},{48,40},{56,32},{64,88... | collective-permute-start | bytes 786440 | tf_op jit(solution)/shard_map/gather_queries/ppermute | solution.py:187
  31.7 0.0 collective-permute-start.8
  31.7 0.0 collective-permute-done.1.refs_1_
  31.7 1.2 %collective-permute-start.9 = (bf16[8,128,128]{2,1,0:T(8,128)(2,1)S(1)}, bf16[8,128,128]{2,1,0:T(8,128)(2,1)S(1)}, u32[]{:S(2)}, u32[]{:S(2)}) collective-permute-start(bf16[8,128,128]{2,1,0:T(8,128)(2,1)S(1)} %all-to-all-done.refs_0_), channel_id=1, source_target_pairs={{0,16},{8,24},{16,0},{24,8},{32,48},{40,56},{48,32},{56,40},{64,80... | collective-permute-start | bytes 786440 | tf_op jit(solution)/shard_map/gather_queries/ppermute | solution.py:187
  32.9 0.9 %collective-permute-done.2.refs_2_ = f32[256,128]{1,0:T(8,128)S(1)} collective-permute-done((f32[256,128]{1,0:T(8,128)S(1)}, f32[256,128]{1,0:T(8,128)S(1)}, u32[]{:S(2)}, u32[]{:S(2)}) %collective-permute-start.2) | collective-permute-done | bytes 131104 | tf_op jit(solution)/shard_map/exchange_tokens/ppermute | solution.py:179
  33.8 2.5 %collective-permute-done.3.refs_3_ = f32[256,128]{1,0:T(8,128)S(1)} collective-permute-done((f32[256,128]{1,0:T(8,128)S(1)}, f32[256,128]{1,0:T(8,128)S(1)}, u32[]{:S(2)}, u32[]{:S(2)}) %collective-permute-start.3) | collective-permute-done | bytes 131104 | tf_op jit(solution)/shard_map/exchange_tokens/ppermute | solution.py:179
  36.3 0.4 outer.1.refs_0_
  36.7 0.0 collective-permute-start.4
  36.7 1.5 %collective-permute-start.5 = (f32[32,128]{1,0:T(8,128)S(1)}, f32[32,128]{1,0:T(8,128)S(1)}, u32[]{:S(2)}, u32[]{:S(2)}) collective-permute-start(f32[32,128]{1,0:T(8,128)S(1)} %outer.1.refs_0_), channel_id=1, source_target_pairs={{0,4},{1,5},{2,6},{3,7},{4,0},{5,1},{6,2},{7,3},{8,12},{9,13},{10,... | collective-permute-start | bytes 49160 | tf_op jit(solution)/shard_map/exchange_grad/ppermute | solution.py:179
  38.2 1.4 %collective-permute-done.4.refs_1_ = f32[32,128]{1,0:T(8,128)S(1)} collective-permute-done((f32[32,128]{1,0:T(8,128)S(1)}, f32[32,128]{1,0:T(8,128)S(1)}, u32[]{:S(2)}, u32[]{:S(2)}) %collective-permute-start.4) | collective-permute-done | bytes 16416 | tf_op jit(solution)/shard_map/exchange_grad/ppermute | solution.py:179
  39.6 1.0 %collective-permute-start.6 = (f32[32,128]{1,0:T(8,128)S(1)}, f32[32,128]{1,0:T(8,128)S(1)}, u32[]{:S(2)}, u32[]{:S(2)}) collective-permute-start(f32[32,128]{1,0:T(8,128)S(1)} %outer.1.refs_0_), channel_id=1, source_target_pairs={{0,6},{1,7},{2,4},{3,5},{4,2},{5,3},{6,0},{7,1},{8,14},{9,15},{10,... | collective-permute-start | bytes 49160 | tf_op jit(solution)/shard_map/exchange_grad/ppermute | solution.py:179
  41.2 0.0 collective-permute-done.5.refs_2_
  41.2 2.4 %collective-permute-done.6.refs_3_ = f32[32,128]{1,0:T(8,128)S(1)} collective-permute-done((f32[32,128]{1,0:T(8,128)S(1)}, f32[32,128]{1,0:T(8,128)S(1)}, u32[]{:S(2)}, u32[]{:S(2)}) %collective-permute-start.6) | collective-permute-done | bytes 16416 | tf_op jit(solution)/shard_map/exchange_grad/ppermute | solution.py:179
  43.7 2.7 %collective-permute-start.7 = (f32[32,128]{1,0:T(8,128)S(1)}, f32[32,128]{1,0:T(8,128)S(1)}, u32[]{:S(2)}, u32[]{:S(2)}) collective-permute-start(f32[32,128]{1,0:T(8,128)S(1)} %sum_parts.1.a_ref), channel_id=1, source_target_pairs={{0,1},{1,0},{2,3},{3,2},{4,5},{5,4},{6,7},{7,6},{8,9},{9,8},{10,11... | collective-permute-start | bytes 49160 | tf_op jit(solution)/shard_map/exchange_grad/ppermute | solution.py:179
  46.4 0.1 pad_add_fusion.ids_ref
  46.4 0.8 %collective-permute-done.7.b_ref = f32[32,128]{1,0:T(8,128)S(1)} collective-permute-done((f32[32,128]{1,0:T(8,128)S(1)}, f32[32,128]{1,0:T(8,128)S(1)}, u32[]{:S(2)}, u32[]{:S(2)}) %collective-permute-start.7) | collective-permute-done | bytes 16416 | tf_op jit(solution)/shard_map/exchange_grad/ppermute | solution.py:179
  47.2 0.0 collective-permute-done.10.refs_3_
  47.2 1.8 %score.1 = f32[1,128]{1,0:T(1,128)} custom-call(s32[3]{0:T(128)S(1)} %pad_add_fusion.ids_ref, f32[32,128]{1,0:T(8,128)S(1)} %sum_parts.1.a_ref, f32[32,128]{1,0:T(8,128)S(1)} %collective-permute-done.7.b_ref, bf16[8,128,128]{2,1,0:T(8,128)(2,1)S(1)} %all-to-all-done.refs_0_, bf16[8,128,128]{2,1,0:T(8,128)(2,1)S(1)} %collective-permute-done.8.refs_1_, ...), custom_call_target="tpu_custom_call" | custom-call | tf_op jit(solution)/shard_map/score/score/pallas_call | solution.py:158
  (9 shorter events, 0.0 us)
Async XLA Ops:
  0.0 9.4 %copy-start.1 = (bf16[128,128]{1,0:T(8,128)(2,1)S(1)}, bf16[128,128]{1,0:T(8,128)(2,1)}, u32[]{:S(2)}) copy-start(bf16[128,128]{1,0:T(8,128)(2,1)} %param.13) | copy-start | bytes 98308
  6.1 26.8 %copy-start.2 = (s32[2048]{0:T(1024)S(1)}, s32[2048]{0:T(1024)}, u32[]{:S(2)}) copy-start(s32[2048]{0:T(1024)} %param.11) | copy-start | bytes 24580
  6.1 16.6 %collective-permute-start = (f32[1024,128]{1,0:T(8,128)}, f32[1024,128]{1,0:T(8,128)S(1)}, u32[]{:S(2)}, u32[]{:S(2)}) collective-permute-start(f32[1024,128]{1,0:T(8,128)} %project.3), channel_id=1, source_target_pairs={{0,1},{1,0},{2,3},{3,2},{4,5},{5,4},{6,7},{7,6},{8,9},{9,8},{10,11... | collective-permute-start | bytes 1572872 | tf_op jit(solution)/shard_map/project/ppermute | solution.py:179
  10.1 18.8 %all-to-all-start = ((bf16[8,128,128]{2,1,0:T(8,128)(2,1)}), bf16[8,128,128]{2,1,0:T(8,128)(2,1)S(1)}, u32[]{:S(2)}, u32[]{:S(2)}) async-start(bf16[8,128,128]{2,1,0:T(8,128)(2,1)} %broadcast_in_dim.10), calls=%async_computation | async-start | bytes 524288 | tf_op jit(solution)/shard_map/gather_queries/all_to_all | solution.py:185
  22.8 1.0 %copy-start = (f32[1024,128]{1,0:T(8,128)S(1)}, f32[1024,128]{1,0:T(8,128)}, u32[]{:S(2)}) copy-start(f32[1024,128]{1,0:T(8,128)} %project.2.a_ref) | copy-start | bytes 1572868
  23.9 7.8 %collective-permute-start.1 = (f32[256,128]{1,0:T(8,128)S(1)}, f32[256,128]{1,0:T(8,128)S(1)}, u32[]{:S(2)}, u32[]{:S(2)}) collective-permute-start(f32[256,128]{1,0:T(8,128)S(1)} %get-tuple-element.10), channel_id=1, source_target_pairs={{0,2},{1,3},{2,0},{3,1},{4,6},{5,7},{6,4},{7,5},{8,10},{9,11},{10,... | collective-permute-start | bytes 393224 | tf_op jit(solution)/shard_map/exchange_tokens/ppermute | solution.py:179
  25.2 8.6 %collective-permute-start.2 = (f32[256,128]{1,0:T(8,128)S(1)}, f32[256,128]{1,0:T(8,128)S(1)}, u32[]{:S(2)}, u32[]{:S(2)}) collective-permute-start(f32[256,128]{1,0:T(8,128)S(1)} %get-tuple-element.11), channel_id=1, source_target_pairs={{0,4},{1,5},{2,6},{3,7},{4,0},{5,1},{6,2},{7,3},{8,12},{9,13},{10,... | collective-permute-start | bytes 393224 | tf_op jit(solution)/shard_map/exchange_tokens/ppermute | solution.py:179
  27.6 8.7 %collective-permute-start.3 = (f32[256,128]{1,0:T(8,128)S(1)}, f32[256,128]{1,0:T(8,128)S(1)}, u32[]{:S(2)}, u32[]{:S(2)}) collective-permute-start(f32[256,128]{1,0:T(8,128)S(1)} %get-tuple-element.12), channel_id=1, source_target_pairs={{0,6},{1,7},{2,4},{3,5},{4,2},{5,3},{6,0},{7,1},{8,14},{9,15},{10,... | collective-permute-start | bytes 393224 | tf_op jit(solution)/shard_map/exchange_tokens/ppermute | solution.py:179
  29.0 18.2 %collective-permute-start.10 = (bf16[8,128,128]{2,1,0:T(8,128)(2,1)S(1)}, bf16[8,128,128]{2,1,0:T(8,128)(2,1)S(1)}, u32[]{:S(2)}, u32[]{:S(2)}) collective-permute-start(bf16[8,128,128]{2,1,0:T(8,128)(2,1)S(1)} %all-to-all-done.refs_0_), channel_id=1, source_target_pairs={{0,24},{8,16},{16,8},{24,0},{32,56},{40,48},{48,40},{56,32},{64,88... | collective-permute-start | bytes 786440 | tf_op jit(solution)/shard_map/gather_queries/ppermute | solution.py:187
  31.7 15.5 %collective-permute-start.8 = (bf16[8,128,128]{2,1,0:T(8,128)(2,1)S(1)}, bf16[8,128,128]{2,1,0:T(8,128)(2,1)S(1)}, u32[]{:S(2)}, u32[]{:S(2)}) collective-permute-start(bf16[8,128,128]{2,1,0:T(8,128)(2,1)S(1)} %all-to-all-done.refs_0_), channel_id=1, source_target_pairs={{0,8},{8,0},{16,24},{24,16},{32,40},{40,32},{48,56},{56,48},{64,72... | collective-permute-start | bytes 786440 | tf_op jit(solution)/shard_map/gather_queries/ppermute | solution.py:187
  31.7 15.5 %collective-permute-start.9 = (bf16[8,128,128]{2,1,0:T(8,128)(2,1)S(1)}, bf16[8,128,128]{2,1,0:T(8,128)(2,1)S(1)}, u32[]{:S(2)}, u32[]{:S(2)}) collective-permute-start(bf16[8,128,128]{2,1,0:T(8,128)(2,1)S(1)} %all-to-all-done.refs_0_), channel_id=1, source_target_pairs={{0,16},{8,24},{16,0},{24,8},{32,48},{40,56},{48,32},{56,40},{64,80... | collective-permute-start | bytes 786440 | tf_op jit(solution)/shard_map/gather_queries/ppermute | solution.py:187
  36.7 2.9 %collective-permute-start.4 = (f32[32,128]{1,0:T(8,128)S(1)}, f32[32,128]{1,0:T(8,128)S(1)}, u32[]{:S(2)}, u32[]{:S(2)}) collective-permute-start(f32[32,128]{1,0:T(8,128)S(1)} %outer.1.refs_0_), channel_id=1, source_target_pairs={{0,2},{1,3},{2,0},{3,1},{4,6},{5,7},{6,4},{7,5},{8,10},{9,11},{10,... | collective-permute-start | bytes 49160 | tf_op jit(solution)/shard_map/exchange_grad/ppermute | solution.py:179
  36.7 4.5 %collective-permute-start.5 = (f32[32,128]{1,0:T(8,128)S(1)}, f32[32,128]{1,0:T(8,128)S(1)}, u32[]{:S(2)}, u32[]{:S(2)}) collective-permute-start(f32[32,128]{1,0:T(8,128)S(1)} %outer.1.refs_0_), channel_id=1, source_target_pairs={{0,4},{1,5},{2,6},{3,7},{4,0},{5,1},{6,2},{7,3},{8,12},{9,13},{10,... | collective-permute-start | bytes 49160 | tf_op jit(solution)/shard_map/exchange_grad/ppermute | solution.py:179
  39.6 4.1 %collective-permute-start.6 = (f32[32,128]{1,0:T(8,128)S(1)}, f32[32,128]{1,0:T(8,128)S(1)}, u32[]{:S(2)}, u32[]{:S(2)}) collective-permute-start(f32[32,128]{1,0:T(8,128)S(1)} %outer.1.refs_0_), channel_id=1, source_target_pairs={{0,6},{1,7},{2,4},{3,5},{4,2},{5,3},{6,0},{7,1},{8,14},{9,15},{10,... | collective-permute-start | bytes 49160 | tf_op jit(solution)/shard_map/exchange_grad/ppermute | solution.py:179
  43.7 3.5 %collective-permute-start.7 = (f32[32,128]{1,0:T(8,128)S(1)}, f32[32,128]{1,0:T(8,128)S(1)}, u32[]{:S(2)}, u32[]{:S(2)}) collective-permute-start(f32[32,128]{1,0:T(8,128)S(1)} %sum_parts.1.a_ref), channel_id=1, source_target_pairs={{0,1},{1,0},{2,3},{3,2},{4,5},{5,4},{6,7},{7,6},{8,9},{9,8},{10,11... | collective-permute-start | bytes 49160 | tf_op jit(solution)/shard_map/exchange_grad/ppermute | solution.py:179
